TPU v7x, 512 devices: a whole 4x4x16 slice. The times are simulated.
512 devices in a mesh: shard: 8 (over x, core), grp: 64 (over z, y).
Axes of the slice: x: 4, y: 4, z: 16, core: 2. Of those that a mesh axis runs over, the one named last changes fastest.
Arguments:
- embeddings: bfloat16 [131072, 768], P(('shard', 'grp')), parts along dimension 0, may hold values from -6 to 6
- cluster_ids: int32 [131072, 1], P(('shard', 'grp')), parts along dimension 0, may hold values from 0 to 127; in each aligned block of 256 rows (0 to 255, 256 to 511, ...) at most 4 rows name the same one
- ranks: int32 [131072], P(('shard', 'grp')), parts along dimension 0, may hold values from 0 to 16383, each once
Outputs:
- best_sim: float32 [131072], P(('shard', 'grp')), parts along dimension 0
There are 8 independent parts, one for each index of `shard`. A program takes and returns all parts, laid end to end along the dimension named above; each array names one. Nothing has to cross between parts.
Inputs may be any that keep to these rules, and one draw needn't show every extreme that they name: `cluster_ids`: among the rows of one device no cluster is named by more than 4 rows, a bound that some block reaches. `ranks`: every value occurs once.
All inputs are finite; a program needn't handle non-finite values.
Results may differ from a plain program's by a relative error of at most 0.0013.
Values may be sent and summed in bfloat16 or wider, within the bound.
No kernel may reach another device: no remote copies, remote signals or barrier semaphores. Data moves between devices by JAX's collectives and lax.ppermute only.
A program may use at most 64 MiB of HBM per device.

v0:
```python
import jax
import jax.numpy as jnp
from jax import lax
from jax.sharding import PartitionSpec as P

CLUS_DEV = 2


def rank_value(digit_high, digit_mid, digit_low):
    return (
        digit_high.astype(jnp.int32) * 65536
        + digit_mid.astype(jnp.int32) * 256
        + digit_low.astype(jnp.int32)
        - 1
    )


def dense_scores(unit_rows, rank_of):
    products = lax.dot_general(
        unit_rows, unit_rows, (((1,), (1,)), ((), ())), preferred_element_type=jnp.float32
    )
    allowed = (rank_of[None, :] < rank_of[:, None]) & (rank_of[None, :] >= 0)
    return jnp.max(jnp.where(allowed, products, jnp.float32(-1.0)), axis=1)


def owner_scores(pieces):
    unit_rows, digit_high, digit_mid, digit_low = pieces
    rank_of = rank_value(digit_high[0], digit_mid[0], digit_low[0])

    def per_item(item):
        return dense_scores(item[0], item[1])

    return lax.map(per_item, (unit_rows[0], rank_of))[None]


def local(embeddings, cluster_ids, ranks):
    groups = lax.axis_size("grp")
    row_count = embeddings.shape[0]
    feature_count = embeddings.shape[1]
    clusters = CLUS_DEV * groups
    slot_cap = 2 * row_count // clusters
    floats = embeddings.astype(jnp.float32)
    unit_rows = (
        floats * lax.rsqrt(jnp.sum(floats * floats, axis=1, keepdims=True) + 1e-06)
    ).astype(jnp.bfloat16)
    cluster_of = cluster_ids[:, 0]
    one_hot = cluster_of[:, None] == jnp.arange(clusters, dtype=jnp.int32)[None, :]
    position = jnp.arange(row_count, dtype=jnp.int32)
    lower = (position[:, None] >= position[None, :]).astype(jnp.bfloat16)
    running = jnp.dot(lower, one_hot.astype(jnp.bfloat16), preferred_element_type=jnp.float32)
    within = jnp.sum(running * one_hot.astype(jnp.float32), axis=1).astype(jnp.int32) - 1
    slot_index = cluster_of * slot_cap + within
    send_rows = (
        jnp.zeros((clusters * slot_cap, feature_count), jnp.bfloat16).at[slot_index].set(unit_rows)
    )
    send_rows = send_rows.reshape(groups, CLUS_DEV, slot_cap, feature_count)
    coded = ranks + 1

    def place_digit(values):
        filled = (
            jnp.zeros((clusters * slot_cap,), jnp.bfloat16)
            .at[slot_index]
            .set(values.astype(jnp.bfloat16))
        )
        return filled.reshape(groups, CLUS_DEV, slot_cap)

    digit_high = place_digit(coded // 65536)
    digit_mid = place_digit(coded // 256 % 256)
    digit_low = place_digit(coded % 256)
    received = (
        lax.all_to_all(send_rows, "grp", split_axis=0, concat_axis=2, tiled=True),
        lax.all_to_all(digit_high, "grp", split_axis=0, concat_axis=2, tiled=True),
        lax.all_to_all(digit_mid, "grp", split_axis=0, concat_axis=2, tiled=True),
        lax.all_to_all(digit_low, "grp", split_axis=0, concat_axis=2, tiled=True),
    )
    scored = owner_scores(received)
    returned = lax.all_to_all(scored, "grp", split_axis=2, concat_axis=0, tiled=True)
    return returned.reshape(-1)[slot_index]


def solution(mesh):
    in_specs = (P(("shard", "grp"), None), P(("shard", "grp"), None), P(("shard", "grp")))
    out_specs = P(("shard", "grp"))
    return jax.shard_map(local, mesh=mesh, in_specs=in_specs, out_specs=out_specs, check_vma=False)
```

profile of v0, /device:TPU:6, one launch (start us, length us, event | category | flops | bytes accessed | tf_op | source)
XLA Modules:
  0.0 149.2 jit_solution(16099191352884118263)
XLA Ops:
  0.0 0.0 copy-start.1
  0.0 0.0 copy-start
  0.0 0.7 copy-done.1
  0.7 0.2 fusion.4
  0.9 0.7 fusion.15
  1.6 2.2 %scatter_custom_fusion = bf16[512]{0:T(512)(128)(2,1)S(1)} fusion(s32[256]{0:T(256)S(1)} %bitcast.35, bf16[256]{0:T(256)(128)(2,1)S(1)} %get-tuple-element.54, bf16[]{:T(256)} %constant.70.clone.1), kind=kCustom, calls=%fused_computation.51 | custom fusion | bytes 1026 | tf_op jit(solution)/shard_map/scatter | solution.py:63
  3.8 0.7 reshape.58
  4.5 18.7 %all-to-all-start = ((bf16[64,2,4]{2,1,0:T(2,128)(2,1)}), bf16[64,2,4]{2,1,0:T(2,128)(2,1)S(1)}, u32[]{:S(2)}, u32[]{:S(2)}) async-start(bf16[64,2,4]{2,1,0:T(2,128)(2,1)} %reshape.58), calls=%async_computation | async-start | bytes 65536 | tf_op jit(solution)/shard_map/all_to_all | solution.py:72
  23.3 2.2 %scatter_custom_fusion.1 = bf16[512]{0:T(512)(128)(2,1)S(1)} fusion(s32[256]{0:T(256)S(1)} %bitcast.36, bf16[256]{0:T(256)(128)(2,1)S(1)} %get-tuple-element.55, bf16[]{:T(256)} %constant.70.clone.1), kind=kCustom, calls=%fused_computation.49 | custom fusion | bytes 1026 | tf_op jit(solution)/shard_map/scatter | solution.py:63
  25.4 0.7 reshape.59
  26.2 11.9 %all-to-all-done = bf16[64,2,4]{2,1,0:T(2,128)(2,1)S(1)} async-done(((bf16[64,2,4]{2,1,0:T(2,128)(2,1)}), bf16[64,2,4]{2,1,0:T(2,128)(2,1)S(1)}, u32[]{:S(2)}, u32[]{:S(2)}) %all-to-all-start) | async-done | bytes 1056 | tf_op jit(solution)/shard_map/all_to_all | solution.py:72
  38.0 4.6 %all-to-all-start.1 = ((bf16[64,2,4]{2,1,0:T(2,128)(2,1)}), bf16[64,2,4]{2,1,0:T(2,128)(2,1)S(1)}, u32[]{:S(2)}, u32[]{:S(2)}) async-start(bf16[64,2,4]{2,1,0:T(2,128)(2,1)} %reshape.59), calls=%async_computation.1 | async-start | bytes 65536 | tf_op jit(solution)/shard_map/all_to_all | solution.py:73
  42.6 0.0 copy-done
  42.7 0.2 fusion.5
  42.8 2.2 %scatter_custom_fusion.2 = bf16[512]{0:T(512)(128)(2,1)S(1)} fusion(s32[256]{0:T(256)S(1)} %bitcast.37, bf16[256]{0:T(256)(128)(2,1)S(1)} %get-tuple-element.56, bf16[]{:T(256)} %constant.70.clone.1), kind=kCustom, calls=%fused_computation.47 | custom fusion | bytes 1026 | tf_op jit(solution)/shard_map/scatter | solution.py:63
  45.0 0.7 reshape.60
  45.7 11.7 %all-to-all-done.1 = bf16[64,2,4]{2,1,0:T(2,128)(2,1)S(1)} async-done(((bf16[64,2,4]{2,1,0:T(2,128)(2,1)}), bf16[64,2,4]{2,1,0:T(2,128)(2,1)S(1)}, u32[]{:S(2)}, u32[]{:S(2)}) %all-to-all-start.1) | async-done | bytes 1056 | tf_op jit(solution)/shard_map/all_to_all | solution.py:73
  57.4 4.6 %all-to-all-start.2 = ((bf16[64,2,4]{2,1,0:T(2,128)(2,1)}), bf16[64,2,4]{2,1,0:T(2,128)(2,1)S(1)}, u32[]{:S(2)}, u32[]{:S(2)}) async-start(bf16[64,2,4]{2,1,0:T(2,128)(2,1)} %reshape.60), calls=%async_computation.2 | async-start | bytes 65536 | tf_op jit(solution)/shard_map/all_to_all | solution.py:74
  62.0 2.0 %scatter_custom_fusion.3 = bf16[512,768]{1,0:T(8,128)(2,1)S(1)} fusion(s32[256]{0:T(256)S(1)} %bitcast.38, bf16[256,768]{1,0:T(8,128)(2,1)S(1)} %copy-done, f32[256]{0:T(256)S(1)} %add_rsqrt_fusion, bf16[]{:T(256)} %constant.70.clone.1), kind=kCustom, calls=%fused_computation.18 | custom fusion | flops 589824 | bytes 1180674 | tf_op jit(solution)/shard_map/scatter | solution.py:54
  64.0 1.1 reshape.61
  65.1 11.7 %all-to-all-done.2 = bf16[64,2,4]{2,1,0:T(2,128)(2,1)S(1)} async-done(((bf16[64,2,4]{2,1,0:T(2,128)(2,1)}), bf16[64,2,4]{2,1,0:T(2,128)(2,1)S(1)}, u32[]{:S(2)}, u32[]{:S(2)}) %all-to-all-start.2) | async-done | bytes 1056 | tf_op jit(solution)/shard_map/all_to_all | solution.py:74
  76.7 4.8 %all-to-all-start.3 = ((bf16[64,2,4,768]{3,2,1,0:T(4,128)(2,1)}), bf16[64,2,4,768]{3,2,1,0:T(4,128)(2,1)S(1)}, u32[]{:S(2)}, u32[]{:S(2)}) async-start(bf16[64,2,4,768]{3,2,1,0:T(4,128)(2,1)} %reshape.61), calls=%async_computation.3 | async-start | bytes 1572864 | tf_op jit(solution)/shard_map/all_to_all | solution.py:71
  81.6 0.1 copy.25
  81.7 0.1 copy.26
  81.8 0.1 copy.27
  81.9 0.1 copy.28
  82.0 0.1 reshape.65
  82.1 39.5 %all-to-all-done.3 = bf16[64,2,4,768]{3,2,1,0:T(4,128)(2,1)S(1)} async-done(((bf16[64,2,4,768]{3,2,1,0:T(4,128)(2,1)}), bf16[64,2,4,768]{3,2,1,0:T(4,128)(2,1)S(1)}, u32[]{:S(2)}, u32[]{:S(2)}) %all-to-all-start.3) | async-done | bytes 786464 | tf_op jit(solution)/shard_map/all_to_all | solution.py:71
  121.6 0.6 copy.29
  122.3 0.1 copy.30
  122.4 0.8 while.10
  122.4 0.3 fusion.25
  122.8 0.3 fusion.25
  123.2 0.8 copy.31
  124.0 5.9 %all-to-all-start.4 = ((f32[1,2,256]{1,0,2:T(1,128)}), f32[1,2,256]{1,0,2:T(1,128)S(1)}, u32[]{:S(2)}, u32[]{:S(2)}) async-start(f32[1,2,256]{1,0,2:T(1,128)} %bitcast.11), calls=%async_computation.4 | async-start | bytes 262144 | tf_op jit(solution)/shard_map/all_to_all | solution.py:77
  129.8 16.1 %all-to-all-done.4 = f32[1,2,256]{1,0,2:T(1,128)S(1)} async-done(((f32[1,2,256]{1,0,2:T(1,128)}), f32[1,2,256]{1,0,2:T(1,128)S(1)}, u32[]{:S(2)}, u32[]{:S(2)}) %all-to-all-start.4) | async-done | bytes 2080 | tf_op jit(solution)/shard_map/all_to_all | solution.py:77
  146.0 0.5 copy.34
  146.5 0.1 copy.33
  146.6 0.1 reshape.62
  146.7 2.5 %gather_fusion = f32[256]{0:T(256)} fusion(f32[512]{0:T(512)S(1)} %reshape.62, s32[1024]{0:T(1024)S(1)} %pad_clamp_fusion), kind=kCustom, calls=%fused_computation | custom fusion | bytes 3072 | tf_op jit(solution)/shard_map/gather | solution.py:78
  (10 shorter events, 0.2 us)
Async XLA Ops:
  0.0 0.7 copy-start.1
  0.0 42.6 %copy-start = (bf16[256,768]{1,0:T(8,128)(2,1)S(1)}, bf16[256,768]{1,0:T(8,128)(2,1)}, u32[]{:S(2)}) copy-start(bf16[256,768]{1,0:T(8,128)(2,1)} %param.5) | copy-start | bytes 1179652
  4.5 33.5 %all-to-all-start = ((bf16[64,2,4]{2,1,0:T(2,128)(2,1)}), bf16[64,2,4]{2,1,0:T(2,128)(2,1)S(1)}, u32[]{:S(2)}, u32[]{:S(2)}) async-start(bf16[64,2,4]{2,1,0:T(2,128)(2,1)} %reshape.58), calls=%async_computation | async-start | bytes 65536 | tf_op jit(solution)/shard_map/all_to_all | solution.py:72
  38.0 19.4 %all-to-all-start.1 = ((bf16[64,2,4]{2,1,0:T(2,128)(2,1)}), bf16[64,2,4]{2,1,0:T(2,128)(2,1)S(1)}, u32[]{:S(2)}, u32[]{:S(2)}) async-start(bf16[64,2,4]{2,1,0:T(2,128)(2,1)} %reshape.59), calls=%async_computation.1 | async-start | bytes 65536 | tf_op jit(solution)/shard_map/all_to_all | solution.py:73
  57.4 19.3 %all-to-all-start.2 = ((bf16[64,2,4]{2,1,0:T(2,128)(2,1)}), bf16[64,2,4]{2,1,0:T(2,128)(2,1)S(1)}, u32[]{:S(2)}, u32[]{:S(2)}) async-start(bf16[64,2,4]{2,1,0:T(2,128)(2,1)} %reshape.60), calls=%async_computation.2 | async-start | bytes 65536 | tf_op jit(solution)/shard_map/all_to_all | solution.py:74
  76.7 44.9 %all-to-all-start.3 = ((bf16[64,2,4,768]{3,2,1,0:T(4,128)(2,1)}), bf16[64,2,4,768]{3,2,1,0:T(4,128)(2,1)S(1)}, u32[]{:S(2)}, u32[]{:S(2)}) async-start(bf16[64,2,4,768]{3,2,1,0:T(4,128)(2,1)} %reshape.61), calls=%async_computation.3 | async-start | bytes 1572864 | tf_op jit(solution)/shard_map/all_to_all | solution.py:71
  124.0 22.0 %all-to-all-start.4 = ((f32[1,2,256]{1,0,2:T(1,128)}), f32[1,2,256]{1,0,2:T(1,128)S(1)}, u32[]{:S(2)}, u32[]{:S(2)}) async-start(f32[1,2,256]{1,0,2:T(1,128)} %bitcast.11), calls=%async_computation.4 | async-start | bytes 262144 | tf_op jit(solution)/shard_map/all_to_all | solution.py:77
where the time goes:
time: 150 us; the launch traced here: 149 us
  waiting for transfers between devices  90.9 us (61%)
  starting transfers between devices  38.6 us (26%)
  local copies, waits for them, and re-layouts  15.7 us (10%)
  other arithmetic  2.92 us (2%)
    all_to_all x1, waiting for transfers between devices, local(): lax.all_to_all(send_rows, 'grp', split_axis=0, concat_axis=2, tiled=True)  39.5 us
    all_to_all x1, starting transfers between devices, local(): lax.all_to_all(digit_high, 'grp', split_axis=0, concat_axis=2, tiled=True)  18.7 us
    all_to_all x1, waiting for transfers between devices, local(): lax.all_to_all(scored, 'grp', split_axis=2, concat_axis=0, tiled=True)  16.1 us
    all_to_all x1, waiting for transfers between devices, local(): lax.all_to_all(digit_high, 'grp', split_axis=0, concat_axis=2, tiled=True)  11.9 us
    all_to_all x1, waiting for transfers between devices, local(): lax.all_to_all(digit_mid, 'grp', split_axis=0, concat_axis=2, tiled=True)  11.7 us
    all_to_all x1, waiting for transfers between devices, local(): lax.all_to_all(digit_low, 'grp', split_axis=0, concat_axis=2, tiled=True)  11.7 us
    scatter x3, local copies, waits for them, and re-layouts, place_digit(): filled = jnp.zeros((clusters * slot_cap,), jnp.bfloat16).at[slot_index].s...  6.48 us
    all_to_all x1, starting transfers between devices, local(): lax.all_to_all(scored, 'grp', split_axis=2, concat_axis=0, tiled=True)  5.87 us
  transfers between devices with their start and end apart: 5, of which 5 were waited for; matrix products, arithmetic and copies ran while one was open for 6% of the time, Pallas kernels for 0%

commit v1 on v0

v1 whole, which is shorter than its diff:
```python
import jax
import jax.numpy as jnp
from jax import lax
from jax.experimental import pallas as pl
from jax.experimental.pallas import tpu as pltpu
from jax.sharding import PartitionSpec as P

CLUS_DEV = 2
DIGIT = 128
TAIL = 128


def slots_of(cluster_row, clusters, slot_cap):
    rows = cluster_row.shape[1]
    cluster = lax.broadcasted_iota(jnp.int32, (clusters, rows), 0)
    one_hot = cluster == cluster_row
    before = lax.broadcasted_iota(jnp.int32, (rows, rows), 0) < lax.broadcasted_iota(jnp.int32, (rows, rows), 1)
    running = jnp.dot(
        one_hot.astype(jnp.bfloat16), before.astype(jnp.bfloat16), preferred_element_type=jnp.float32
    )
    within = jnp.sum(jnp.where(one_hot, running, 0.0), axis=0, keepdims=True).astype(jnp.int32)
    return cluster_row * slot_cap + within


def pack_kernel(clusters, slot_cap, rows_ref, cluster_ref, rank_ref, send_ref):
    rows, features = rows_ref.shape
    groups, slots, width = send_ref.shape
    floats = rows_ref[...].astype(jnp.float32)
    unit = (floats * lax.rsqrt(jnp.sum(floats * floats, axis=1, keepdims=True) + 1e-06)).astype(jnp.bfloat16)
    slot_row = slots_of(cluster_ref[...], clusters, slot_cap)
    place = (lax.broadcasted_iota(jnp.int32, (groups * slots, rows), 0) == slot_row).astype(jnp.bfloat16)
    placed = jnp.dot(place, unit, preferred_element_type=jnp.float32)
    send_ref[:, :, :features] = placed.reshape(groups, slots, features).astype(jnp.bfloat16)
    rank_row = rank_ref[...]
    line = lax.broadcasted_iota(jnp.int32, (width - features, rows), 0)
    high = rank_row // DIGIT
    digits = jnp.where(line == 0, high + 1, jnp.where(line == 1, rank_row - high * DIGIT, 0))
    placed_digits = lax.dot_general(
        place,
        digits.astype(jnp.float32).astype(jnp.bfloat16),
        (((1,), (1,)), ((), ())),
        preferred_element_type=jnp.float32,
    )
    send_ref[:, :, features:] = placed_digits.reshape(groups, slots, width - features).astype(jnp.bfloat16)


def score_kernel(slot_cap, features, got_ref, best_ref):
    groups, slots, width = got_ref.shape
    count = groups * slots
    unit = got_ref[:, :, :features].astype(jnp.float32).reshape(count, features).astype(jnp.bfloat16)
    digits = got_ref[:, :, features:].astype(jnp.float32).reshape(count, width - features).astype(jnp.bfloat16)
    lane = lax.broadcasted_iota(jnp.int32, (8, width - features), 1)
    weight = jnp.where(lane == 0, DIGIT, jnp.where(lane == 1, 1, 0)).astype(jnp.float32).astype(jnp.bfloat16)
    dims = (((1,), (1,)), ((), ()))
    rank_row = lax.dot_general(weight, digits, dims, preferred_element_type=jnp.float32)[0:1, :]
    rank_col = lax.dot_general(digits, weight, dims, preferred_element_type=jnp.float32)[:, 0:1]
    products = lax.dot_general(unit, unit, dims, preferred_element_type=jnp.float32)
    cluster_row = lax.broadcasted_iota(jnp.int32, (1, count), 1) % slots // slot_cap
    cluster_col = lax.broadcasted_iota(jnp.int32, (count, 1), 0) % slots // slot_cap
    empty = rank_row < DIGIT
    rank_row = jnp.where(empty, jnp.float32(1e9), rank_row)
    allowed = (rank_row < rank_col) & (cluster_row == cluster_col)
    best = jnp.max(jnp.where(allowed, products, jnp.float32(-1.0)), axis=1, keepdims=True)
    spread = lax.broadcasted_iota(jnp.int32, (count, 128), 1) == lax.broadcasted_iota(jnp.int32, (count, 128), 0) % slots
    lines = jnp.where(spread, best, 0.0).reshape(groups, slots, 128)
    best_ref[...] = jnp.sum(lines, axis=1)


def pick_kernel(clusters, slot_cap, back_ref, cluster_ref, out_ref):
    groups, width = back_ref.shape
    rows = cluster_ref.shape[1]
    slots = CLUS_DEV * slot_cap
    slot_row = slots_of(cluster_ref[...], clusters, slot_cap)
    owner_row = slot_row // slots
    owner = (lax.broadcasted_iota(jnp.int32, (groups, rows), 0) == owner_row).astype(jnp.float32)
    lines = lax.dot_general(
        back_ref[...],
        owner,
        (((0,), (0,)), ((), ())),
        precision=lax.Precision.HIGHEST,
        preferred_element_type=jnp.float32,
    )
    mine = lax.broadcasted_iota(jnp.int32, (width, rows), 0) == slot_row - owner_row * slots
    out_ref[...] = jnp.sum(jnp.where(mine, lines, 0.0), axis=0, keepdims=True)


def local(embeddings, cluster_ids, ranks):
    groups = lax.axis_size("grp")
    rows, features = embeddings.shape
    clusters = CLUS_DEV * groups
    slot_cap = 2 * rows // clusters
    slots = CLUS_DEV * slot_cap
    cluster_row = cluster_ids.reshape(1, rows)
    rank_row = ranks.reshape(1, rows)
    params = pltpu.CompilerParams(vmem_limit_bytes=48 * 1024 * 1024)

    def pack(*refs):
        pack_kernel(clusters, slot_cap, *refs)

    def score(*refs):
        score_kernel(slot_cap, features, *refs)

    def pick(*refs):
        pick_kernel(clusters, slot_cap, *refs)

    send = pl.pallas_call(
        pack,
        out_shape=jax.ShapeDtypeStruct((groups, slots, features + TAIL), jnp.bfloat16),
        compiler_params=params,
        name="pack_rows",
    )(embeddings, cluster_row, rank_row)
    got = lax.all_to_all(send, "grp", split_axis=0, concat_axis=0, tiled=True)
    best = pl.pallas_call(
        score,
        out_shape=jax.ShapeDtypeStruct((groups, 128), jnp.float32),
        compiler_params=params,
        name="score_rows",
    )(got)
    back = lax.all_to_all(best, "grp", split_axis=0, concat_axis=0, tiled=True)
    out = pl.pallas_call(
        pick,
        out_shape=jax.ShapeDtypeStruct((1, rows), jnp.float32),
        compiler_params=params,
        name="pick_rows",
    )(back, cluster_row)
    return out.reshape(rows)


def solution(mesh):
    in_specs = (P(("shard", "grp"), None), P(("shard", "grp"), None), P(("shard", "grp")))
    out_specs = P(("shard", "grp"))
    return jax.shard_map(local, mesh=mesh, in_specs=in_specs, out_specs=out_specs, check_vma=False)
```

time: 150 us -> 92.9 us (0.62)
  waiting for transfers between devices: 90.9 us -> 0 us
  blocking collectives: 0 us -> 88.5 us
  starting transfers between devices: 38.6 us -> 0 us
  local copies, waits for them, and re-layouts: 15.7 us -> 1.69 us
  other arithmetic: 2.92 us -> 0 us
  Pallas kernels: 0 us -> 2.5 us
    all_to_all x5 -> x0, waiting for transfers between devices: 90.9 us -> none  [the longest x1 39.5 us: local(): lax.all_to_all(send_rows, 'grp', split_axis=0, concat_axis=2, tiled=True)]
    all_to_all x0 -> x2, blocking collectives: none -> 88.5 us  [the longest x1 68.2 us: local(): got = lax.all_to_all(send, 'grp', split_axis=0, concat_axis=0, tiled=True)]
    all_to_all x5 -> x0, starting transfers between devices: 38.6 us -> none  [the longest x1 18.7 us: local(): lax.all_to_all(digit_high, 'grp', split_axis=0, concat_axis=2, tiled=True)]
    scatter x3 -> x0, local copies, waits for them, and re-layouts: 6.48 us -> none  [place_digit(): filled = jnp.zeros((clusters * slot_cap,), jnp.bfloat16).at[slot_index].s...]
    reshape x5 -> x0, local copies, waits for them, and re-layouts: 3.35 us -> none  [the longest x3 2.17 us: place_digit(): return filled.reshape(groups, CLUS_DEV, slot_cap)]
    gather x1 -> x0, local copies, waits for them, and re-layouts: 2.51 us -> none  [local(): return returned.reshape(-1)[slot_index]]
    pallas_call x0 -> x3, Pallas kernels: none -> 2.5 us  [the longest x1 1.06 us: local(): pl.pallas_call(pick, out_shape=jax.ShapeDtypeStruct((1, rows), jnp.float3...]
    scatter x1 -> x0, other arithmetic: 1.97 us -> none  [local(): jnp.zeros((clusters * slot_cap, feature_count), jnp.bfloat16).at[slot_index]]
  transfers between devices with their start and end apart: 5 -> 0, of which waited for: 5 -> 0; matrix products, arithmetic and copies ran while one was open for 6% -> 0% of each run, Pallas kernels for 0% -> 0%
where the time goes in v1:
time: 92.9 us; the launch traced here: 92.7 us
  blocking collectives  88.5 us (95%)
  Pallas kernels  2.5 us (3%)
  local copies, waits for them, and re-layouts  1.69 us (2%)
    all_to_all x1, blocking collectives, local(): got = lax.all_to_all(send, 'grp', split_axis=0, concat_axis=0, tiled=True)  68.2 us
    all_to_all x1, blocking collectives, local(): back = lax.all_to_all(best, 'grp', split_axis=0, concat_axis=0, tiled=True)  20.2 us

profile of v1, /device:TPU:6, one launch (start us, length us, event | category | flops | bytes accessed | tf_op | source)
XLA Modules:
  0.0 92.7 jit_solution(18402432689963459320)
XLA Ops:
  0.0 0.0 copy-start.2
  0.0 0.0 copy-start.1
  0.0 0.7 copy-done.2
  0.7 0.0 copy-done.1
  0.7 0.0 copy-start
  0.7 1.0 %copy-done = bf16[256,768]{1,0:T(8,128)(2,1)S(1)} copy-done((bf16[256,768]{1,0:T(8,128)(2,1)S(1)}, bf16[256,768]{1,0:T(8,128)(2,1)}, u32[]{:S(2)}) %copy-start) | copy-done | bytes 393240
  1.7 0.6 pack_rows.1
  2.3 68.2 %all_to_all.16.refs_0_ = bf16[64,8,896]{2,1,0:T(8,128)(2,1)S(1)} all-to-all(bf16[64,8,896]{2,1,0:T(8,128)(2,1)S(1)} %pack_rows.1), channel_id=1, replica_groups=mesh['shard'=8,'grp'=64] {'grp'}, dimensions={0} | all-to-all | bytes 1835008 | tf_op jit(solution)/shard_map/all_to_all | solution.py:112
  70.5 0.8 score_rows.1
  71.3 20.2 %all_to_all.17 = f32[64,1,128]{2,1,0:T(1,128)S(1)} all-to-all(f32[64,1,128]{2,1,0:T(1,128)S(1)} %bitcast.8), channel_id=1, replica_groups=mesh['shard'=8,'grp'=64] {'grp'}, dimensions={0} | all-to-all | bytes 65536 | tf_op jit(solution)/shard_map/all_to_all | solution.py:119
  91.6 1.1 %pick_rows.1 = f32[1,256]{1,0:T(1,128)} custom-call(f32[64,128]{1,0:T(8,128)S(1)} %bitcast.7, s32[1,256]{1,0:T(1,128)S(1)} %bitcast.10), custom_call_target="tpu_custom_call" | custom-call | tf_op jit(solution)/shard_map/pick_rows/pallas_call | solution.py:120
Async XLA Ops:
  0.0 0.7 copy-start.2
  0.0 0.7 copy-start.1
  0.7 1.0 %copy-start = (bf16[256,768]{1,0:T(8,128)(2,1)S(1)}, bf16[256,768]{1,0:T(8,128)(2,1)}, u32[]{:S(2)}) copy-start(bf16[256,768]{1,0:T(8,128)(2,1)} %refs_0_.1) | copy-start | bytes 1179652

commit v2 on v1

v2 whole, which is shorter than its diff:
```python
import jax
import jax.numpy as jnp
from jax import lax
from jax.experimental import pallas as pl
from jax.experimental.pallas import tpu as pltpu
from jax.sharding import PartitionSpec as P

CLUS_DEV = 2
DIGIT = 128
LANES = 128


def lines_of(slots, features):
    return slots * (features // LANES) + 2


def slots_of(cluster_row, clusters, slot_cap):
    rows = cluster_row.shape[1]
    cluster = lax.broadcasted_iota(jnp.int32, (clusters, rows), 0)
    one_hot = cluster == cluster_row
    before = lax.broadcasted_iota(jnp.int32, (rows, rows), 0) < lax.broadcasted_iota(jnp.int32, (rows, rows), 1)
    running = jnp.dot(
        one_hot.astype(jnp.bfloat16), before.astype(jnp.bfloat16), preferred_element_type=jnp.float32
    )
    within = jnp.sum(jnp.where(one_hot, running, 0.0), axis=0, keepdims=True).astype(jnp.int32)
    return cluster_row * slot_cap + within


def one_hot_bf16(hit):
    return hit.astype(jnp.float32).astype(jnp.bfloat16)


def pack_kernel(clusters, slot_cap, rows_ref, cluster_ref, rank_ref, send_ref, lines_ref):
    rows, features = rows_ref.shape
    slots = CLUS_DEV * slot_cap
    groups = clusters // CLUS_DEV
    span = lines_of(slots, features)
    floats = rows_ref[...].astype(jnp.float32)
    unit = (floats * lax.rsqrt(jnp.sum(floats * floats, axis=1, keepdims=True) + 1e-06)).astype(jnp.bfloat16)
    slot_row = slots_of(cluster_ref[...], clusters, slot_cap)
    place = one_hot_bf16(lax.broadcasted_iota(jnp.int32, (groups * slots, rows), 0) == slot_row)
    placed = jnp.dot(place, unit, preferred_element_type=jnp.float32)
    for group in range(groups):
        for block in range(features // LANES):
            lines_ref[group * span + block * slots : group * span + (block + 1) * slots, :] = placed[
                group * slots : (group + 1) * slots, block * LANES : (block + 1) * LANES
            ]
    rank_row = rank_ref[...]
    high = rank_row // DIGIT
    owner_row = slot_row // slots
    owned = lax.broadcasted_iota(jnp.int32, (groups, rows), 0) == owner_row
    lane = one_hot_bf16(lax.broadcasted_iota(jnp.int32, (LANES, rows), 0) == slot_row - owner_row * slots)
    for line, digit in enumerate((high + 1, rank_row - high * DIGIT)):
        digits = jnp.where(owned, digit, 0).astype(jnp.float32).astype(jnp.bfloat16)
        lines_ref[pl.ds(span - 2 + line, groups, stride=span), :] = lax.dot_general(
            digits, lane, (((1,), (1,)), ((), ())), preferred_element_type=jnp.float32
        )
    send_ref[...] = lines_ref[...].astype(jnp.bfloat16)


def score_kernel(slot_cap, groups, features, got_ref, best_ref, lines_ref):
    slots = CLUS_DEV * slot_cap
    count = groups * slots
    span = lines_of(slots, features)
    lines_ref[...] = got_ref[...].astype(jnp.float32)
    unit = jnp.concatenate(
        [
            jnp.concatenate(
                [
                    lines_ref[group * span + block * slots : group * span + (block + 1) * slots, :]
                    for group in range(groups)
                ],
                axis=0,
            ).astype(jnp.bfloat16)
            for block in range(features // LANES)
        ],
        axis=1,
    )
    high = lines_ref[pl.ds(span - 2, groups, stride=span), :]
    low = lines_ref[pl.ds(span - 1, groups, stride=span), :]
    spread = lax.broadcasted_iota(jnp.int32, (count, LANES), 1) == lax.broadcasted_iota(jnp.int32, (count, LANES), 0) % slots
    rank = (high * DIGIT + low).reshape(groups, 1, LANES)
    rank = jnp.broadcast_to(rank, (groups, slots, LANES)).reshape(count, LANES)
    rank_col = jnp.sum(jnp.where(spread, rank, 0.0), axis=1, keepdims=True)
    lane = lax.broadcasted_iota(jnp.int32, (LANES, count), 0) == lax.broadcasted_iota(jnp.int32, (LANES, count), 1) % slots
    spread_row = jnp.dot(
        high.astype(jnp.bfloat16), one_hot_bf16(lane) * DIGIT, preferred_element_type=jnp.float32
    ) + jnp.dot(low.astype(jnp.bfloat16), one_hot_bf16(lane), preferred_element_type=jnp.float32)
    mine = lax.broadcasted_iota(jnp.int32, (groups, count), 0) == lax.broadcasted_iota(jnp.int32, (groups, count), 1) // slots
    rank_row = jnp.sum(jnp.where(mine, spread_row, 0.0), axis=0, keepdims=True)
    products = lax.dot_general(unit, unit, (((1,), (1,)), ((), ())), preferred_element_type=jnp.float32)
    cluster_row = lax.broadcasted_iota(jnp.int32, (1, count), 1) % slots // slot_cap
    cluster_col = lax.broadcasted_iota(jnp.int32, (count, 1), 0) % slots // slot_cap
    rank_row = jnp.where(rank_row < DIGIT, jnp.float32(1e9), rank_row)
    allowed = (rank_row < rank_col) & (cluster_row == cluster_col)
    best = jnp.max(jnp.where(allowed, products, jnp.float32(-1.0)), axis=1, keepdims=True)
    best_ref[...] = jnp.sum(jnp.where(spread, best, 0.0).reshape(groups, slots, LANES), axis=1)


def pick_kernel(clusters, slot_cap, back_ref, cluster_ref, out_ref):
    groups, width = back_ref.shape
    rows = cluster_ref.shape[1]
    slots = CLUS_DEV * slot_cap
    slot_row = slots_of(cluster_ref[...], clusters, slot_cap)
    owner_row = slot_row // slots
    owner = (lax.broadcasted_iota(jnp.int32, (groups, rows), 0) == owner_row).astype(jnp.float32)
    lines = lax.dot_general(
        back_ref[...],
        owner,
        (((0,), (0,)), ((), ())),
        precision=lax.Precision.HIGHEST,
        preferred_element_type=jnp.float32,
    )
    mine = lax.broadcasted_iota(jnp.int32, (width, rows), 0) == slot_row - owner_row * slots
    out_ref[...] = jnp.sum(jnp.where(mine, lines, 0.0), axis=0, keepdims=True)


def local(embeddings, cluster_ids, ranks):
    groups = lax.axis_size("grp")
    rows, features = embeddings.shape
    clusters = CLUS_DEV * groups
    slot_cap = 2 * rows // clusters
    slots = CLUS_DEV * slot_cap
    cluster_row = cluster_ids.reshape(1, rows)
    rank_row = ranks.reshape(1, rows)
    params = pltpu.CompilerParams(vmem_limit_bytes=48 * 1024 * 1024)

    def pack(*refs):
        pack_kernel(clusters, slot_cap, *refs)

    def score(*refs):
        score_kernel(slot_cap, groups, features, *refs)

    def pick(*refs):
        pick_kernel(clusters, slot_cap, *refs)

    span = lines_of(slots, features)
    lines = pltpu.VMEM((groups * span, LANES), jnp.float32)
    send = pl.pallas_call(
        pack,
        out_shape=jax.ShapeDtypeStruct((groups * span, LANES), jnp.bfloat16),
        scratch_shapes=[lines],
        compiler_params=params,
        name="pack_rows",
    )(embeddings, cluster_row, rank_row)
    got = lax.all_to_all(
        send.reshape(groups, span // 2, 2, LANES), "grp", split_axis=0, concat_axis=0, tiled=True
    ).reshape(groups * span, LANES)
    best = pl.pallas_call(
        score,
        out_shape=jax.ShapeDtypeStruct((groups, LANES), jnp.float32),
        scratch_shapes=[lines],
        compiler_params=params,
        name="score_rows",
    )(got)
    back = lax.all_to_all(best, "grp", split_axis=0, concat_axis=0, tiled=True)
    out = pl.pallas_call(
        pick,
        out_shape=jax.ShapeDtypeStruct((1, rows), jnp.float32),
        compiler_params=params,
        name="pick_rows",
    )(back, cluster_row)
    return out.reshape(rows)


def solution(mesh):
    in_specs = (P(("shard", "grp"), None), P(("shard", "grp"), None), P(("shard", "grp")))
    out_specs = P(("shard", "grp"))
    return jax.shard_map(local, mesh=mesh, in_specs=in_specs, out_specs=out_specs, check_vma=False)
```

time: 92.9 us -> 88.8 us (0.956)
  blocking collectives: 88.5 us -> 84.2 us
    all_to_all x1, blocking collectives: 68.2 us -> 64 us  [local(): lax.all_to_all(send.reshape(groups, span // 2, 2, LANES), 'grp', split_ax...]
where the time goes in v2:
time: 88.8 us; the launch traced here: 88.6 us
  blocking collectives  84.2 us (95%)
  Pallas kernels  2.69 us (3%)
  local copies, waits for them, and re-layouts  1.69 us (2%)
    all_to_all x1, blocking collectives, local(): lax.all_to_all(send.reshape(groups, span // 2, 2, LANES), 'grp', split_ax...  64 us
    all_to_all x1, blocking collectives, local(): back = lax.all_to_all(best, 'grp', split_axis=0, concat_axis=0, tiled=True)  20.2 us

profile of v2, /device:TPU:6, one launch (start us, length us, event | category | flops | bytes accessed | tf_op | source)
XLA Modules:
  0.0 88.6 jit_solution(8531269739704299628)
XLA Ops:
  0.0 0.0 copy-start.2
  0.0 0.0 copy-start.1
  0.0 0.7 copy-done.2
  0.7 0.0 copy-done.1
  0.7 0.0 copy-start
  0.7 1.0 %copy-done = bf16[256,768]{1,0:T(8,128)(2,1)S(1)} copy-done((bf16[256,768]{1,0:T(8,128)(2,1)S(1)}, bf16[256,768]{1,0:T(8,128)(2,1)}, u32[]{:S(2)}) %copy-start) | copy-done | bytes 393240
  1.7 0.7 pack_rows.1
  2.4 64.0 %all_to_all.16 = bf16[64,25,2,128]{3,2,1,0:T(2,128)(2,1)S(1)} all-to-all(bf16[64,25,2,128]{3,2,1,0:T(2,128)(2,1)S(1)} %bitcast.9), channel_id=1, replica_groups=mesh['shard'=8,'grp'=64] {'grp'}, dimensions={0} | all-to-all | bytes 1638400 | tf_op jit(solution)/shard_map/all_to_all | solution.py:146
  66.4 0.9 %score_rows.1 = f32[64,128]{1,0:T(8,128)S(1)} custom-call(bf16[3200,128]{1,0:T(8,128)(2,1)S(1)} %bitcast.10), custom_call_target="tpu_custom_call" | custom-call | tf_op jit(solution)/shard_map/score_rows/pallas_call | solution.py:149
  67.3 20.2 %all_to_all.17 = f32[64,1,128]{2,1,0:T(1,128)S(1)} all-to-all(f32[64,1,128]{2,1,0:T(1,128)S(1)} %bitcast.12), channel_id=1, replica_groups=mesh['shard'=8,'grp'=64] {'grp'}, dimensions={0} | all-to-all | bytes 65536 | tf_op jit(solution)/shard_map/all_to_all | solution.py:156
  87.6 1.1 %pick_rows.1 = f32[1,256]{1,0:T(1,128)} custom-call(f32[64,128]{1,0:T(8,128)S(1)} %bitcast.11, s32[1,256]{1,0:T(1,128)S(1)} %bitcast.14), custom_call_target="tpu_custom_call" | custom-call | tf_op jit(solution)/shard_map/pick_rows/pallas_call | solution.py:157
Async XLA Ops:
  0.0 0.7 copy-start.2
  0.0 0.7 copy-start.1
  0.7 1.0 %copy-start = (bf16[256,768]{1,0:T(8,128)(2,1)S(1)}, bf16[256,768]{1,0:T(8,128)(2,1)}, u32[]{:S(2)}) copy-start(bf16[256,768]{1,0:T(8,128)(2,1)} %refs_0_.1) | copy-start | bytes 1179652

commit v3 on v2

--- a/solution.py
+++ b/solution.py
@@ -30,21 +30,26 @@
     return hit.astype(jnp.float32).astype(jnp.bfloat16)
 
 
-def pack_kernel(clusters, slot_cap, rows_ref, cluster_ref, rank_ref, send_ref, lines_ref):
+def pack_kernel(
+    clusters, slot_cap, rows_hbm, cluster_hbm, rank_hbm, send_ref, slot_ref, rows_ref, cluster_ref, rank_ref, lines_ref, sems
+):
     rows, features = rows_ref.shape
     slots = CLUS_DEV * slot_cap
     groups = clusters // CLUS_DEV
     span = lines_of(slots, features)
-    floats = rows_ref[...].astype(jnp.float32)
-    unit = (floats * lax.rsqrt(jnp.sum(floats * floats, axis=1, keepdims=True) + 1e-06)).astype(jnp.bfloat16)
+    copies = [
+        pltpu.make_async_copy(source, target, sems.at[index])
+        for index, (source, target) in enumerate(
+            ((cluster_hbm, cluster_ref), (rank_hbm, rank_ref), (rows_hbm, rows_ref))
+        )
+    ]
+    for copy in copies:
+        copy.start()
+    copies[0].wait()
     slot_row = slots_of(cluster_ref[...], clusters, slot_cap)
+    slot_ref[...] = slot_row
     place = one_hot_bf16(lax.broadcasted_iota(jnp.int32, (groups * slots, rows), 0) == slot_row)
-    placed = jnp.dot(place, unit, preferred_element_type=jnp.float32)
-    for group in range(groups):
-        for block in range(features // LANES):
-            lines_ref[group * span + block * slots : group * span + (block + 1) * slots, :] = placed[
-                group * slots : (group + 1) * slots, block * LANES : (block + 1) * LANES
-            ]
+    copies[1].wait()
     rank_row = rank_ref[...]
     high = rank_row // DIGIT
     owner_row = slot_row // slots
@@ -55,6 +60,15 @@
         lines_ref[pl.ds(span - 2 + line, groups, stride=span), :] = lax.dot_general(
             digits, lane, (((1,), (1,)), ((), ())), preferred_element_type=jnp.float32
         )
+    copies[2].wait()
+    floats = rows_ref[...].astype(jnp.float32)
+    unit = (floats * lax.rsqrt(jnp.sum(floats * floats, axis=1, keepdims=True) + 1e-06)).astype(jnp.bfloat16)
+    placed = jnp.dot(place, unit, preferred_element_type=jnp.float32)
+    for group in range(groups):
+        for block in range(features // LANES):
+            lines_ref[group * span + block * slots : group * span + (block + 1) * slots, :] = placed[
+                group * slots : (group + 1) * slots, block * LANES : (block + 1) * LANES
+            ]
     send_ref[...] = lines_ref[...].astype(jnp.bfloat16)
 
 
@@ -97,22 +111,14 @@
     best_ref[...] = jnp.sum(jnp.where(spread, best, 0.0).reshape(groups, slots, LANES), axis=1)
 
 
-def pick_kernel(clusters, slot_cap, back_ref, cluster_ref, out_ref):
-    groups, width = back_ref.shape
-    rows = cluster_ref.shape[1]
-    slots = CLUS_DEV * slot_cap
-    slot_row = slots_of(cluster_ref[...], clusters, slot_cap)
-    owner_row = slot_row // slots
-    owner = (lax.broadcasted_iota(jnp.int32, (groups, rows), 0) == owner_row).astype(jnp.float32)
-    lines = lax.dot_general(
-        back_ref[...],
-        owner,
-        (((0,), (0,)), ((), ())),
-        precision=lax.Precision.HIGHEST,
-        preferred_element_type=jnp.float32,
-    )
-    mine = lax.broadcasted_iota(jnp.int32, (width, rows), 0) == slot_row - owner_row * slots
-    out_ref[...] = jnp.sum(jnp.where(mine, lines, 0.0), axis=0, keepdims=True)
+def pick_kernel(slots, back_ref, slot_ref, out_ref):
+    groups = back_ref.shape[0]
+    rows = slot_ref.shape[1]
+    ahead = slot_ref[...] - lax.broadcasted_iota(jnp.int32, (groups, rows), 0) * slots
+    picked = jnp.zeros((groups, rows), jnp.float32)
+    for slot in range(slots):
+        picked = jnp.where(ahead == slot, back_ref[:, slot : slot + 1], picked)
+    out_ref[...] = jnp.sum(picked, axis=0, keepdims=True)
 
 
 def local(embeddings, cluster_ids, ranks):
@@ -132,17 +138,27 @@
         score_kernel(slot_cap, groups, features, *refs)
 
     def pick(*refs):
-        pick_kernel(clusters, slot_cap, *refs)
+        pick_kernel(slots, *refs)
 
     span = lines_of(slots, features)
     lines = pltpu.VMEM((groups * span, LANES), jnp.float32)
-    send = pl.pallas_call(
+    send, slot_row = pl.pallas_call(
         pack,
-        out_shape=jax.ShapeDtypeStruct((groups * span, LANES), jnp.bfloat16),
-        scratch_shapes=[lines],
+        in_specs=[pl.BlockSpec(memory_space=pltpu.HBM)] * 3,
+        out_shape=(
+            jax.ShapeDtypeStruct((groups * span, LANES), jnp.bfloat16),
+            jax.ShapeDtypeStruct((1, rows), jnp.int32),
+        ),
+        scratch_shapes=[
+            pltpu.VMEM((rows, features), jnp.bfloat16),
+            pltpu.VMEM((1, rows), jnp.int32),
+            pltpu.VMEM((1, rows), jnp.int32),
+            lines,
+            pltpu.SemaphoreType.DMA((3,)),
+        ],
         compiler_params=params,
         name="pack_rows",
-    )(embeddings, cluster_row, rank_row)
+    )(*(pltpu.with_memory_space_constraint(x, pltpu.HBM) for x in (embeddings, cluster_row, rank_row)))
     got = lax.all_to_all(
         send.reshape(groups, span // 2, 2, LANES), "grp", split_axis=0, concat_axis=0, tiled=True
     ).reshape(groups * span, LANES)
@@ -159,7 +175,7 @@
         out_shape=jax.ShapeDtypeStruct((1, rows), jnp.float32),
         compiler_params=params,
         name="pick_rows",
-    )(back, cluster_row)
+    )(back, slot_row)
     return out.reshape(rows)
 
 

time: 88.8 us -> 87.8 us (0.989)
  local copies, waits for them, and re-layouts: 1.69 us -> 0 us
    unnamed x6 -> x0, local copies, waits for them, and re-layouts: 1.69 us -> none
    pallas_call x1, Pallas kernels: 0.72 us -> 1.73 us  [local(): pl.pallas_call(pack, in_specs=[pl.BlockSpec(memory_space=pltpu.HBM)] * 3,...]
where the time goes in v3:
time: 87.8 us; the launch traced here: 87.6 us
  blocking collectives  84.2 us (96%)
  Pallas kernels  3.37 us (4%)
    all_to_all x1, blocking collectives, local(): lax.all_to_all(send.reshape(groups, span // 2, 2, LANES), 'grp', split_ax...  64 us
    all_to_all x1, blocking collectives, local(): back = lax.all_to_all(best, 'grp', split_axis=0, concat_axis=0, tiled=True)  20.2 us

profile of v3, /device:TPU:6, one launch (start us, length us, event | category | flops | bytes accessed | tf_op | source)
XLA Modules:
  0.0 87.6 jit_solution(394189154027831323)
XLA Ops:
  0.0 1.7 %pack_rows.1 = (bf16[3200,128]{1,0:T(8,128)(2,1)S(1)}, s32[1,256]{1,0:T(1,128)S(1)}) custom-call(bf16[256,768]{1,0:T(8,128)(2,1)} %refs_0_.1, s32[1,256]{1,0:T(1,128)} %bitcast.13, s32[1,256]{1,0:T(1,128)} %bitcast.14), custom_call_target="tpu_custom_call" | custom-call | tf_op jit(solution)/shard_map/pack_rows/pallas_call | solution.py:145
  1.7 64.0 %all_to_all.16 = bf16[64,25,2,128]{3,2,1,0:T(2,128)(2,1)S(1)} all-to-all(bf16[64,25,2,128]{3,2,1,0:T(2,128)(2,1)S(1)} %bitcast.10), channel_id=1, replica_groups=mesh['shard'=8,'grp'=64] {'grp'}, dimensions={0} | all-to-all | bytes 1638400 | tf_op jit(solution)/shard_map/all_to_all | solution.py:162
  65.7 0.9 %score_rows.1 = f32[64,128]{1,0:T(8,128)S(1)} custom-call(bf16[3200,128]{1,0:T(8,128)(2,1)S(1)} %bitcast.9), custom_call_target="tpu_custom_call" | custom-call | tf_op jit(solution)/shard_map/score_rows/pallas_call | solution.py:165
  66.6 20.2 %all_to_all.17 = f32[64,1,128]{2,1,0:T(1,128)S(1)} all-to-all(f32[64,1,128]{2,1,0:T(1,128)S(1)} %bitcast.12), channel_id=1, replica_groups=mesh['shard'=8,'grp'=64] {'grp'}, dimensions={0} | all-to-all | bytes 65536 | tf_op jit(solution)/shard_map/all_to_all | solution.py:172
  86.9 0.7 pick_rows.1

commit v4 on v3

--- a/solution.py
+++ b/solution.py
@@ -8,6 +8,7 @@
 CLUS_DEV = 2
 DIGIT = 128
 LANES = 128
+FIRST = 38
 
 
 def lines_of(slots, features):
@@ -140,6 +141,11 @@
     def pick(*refs):
         pick_kernel(slots, *refs)
 
+    order = [[(FIRST + place) % groups for place in range(groups)]]
+
+    def exchange(pieces):
+        return lax.all_to_all(pieces, "grp", split_axis=0, concat_axis=0, axis_index_groups=order, tiled=True)
+
     span = lines_of(slots, features)
     lines = pltpu.VMEM((groups * span, LANES), jnp.float32)
     send, slot_row = pl.pallas_call(
@@ -159,9 +165,7 @@
         compiler_params=params,
         name="pack_rows",
     )(*(pltpu.with_memory_space_constraint(x, pltpu.HBM) for x in (embeddings, cluster_row, rank_row)))
-    got = lax.all_to_all(
-        send.reshape(groups, span // 2, 2, LANES), "grp", split_axis=0, concat_axis=0, tiled=True
-    ).reshape(groups * span, LANES)
+    got = exchange(send.reshape(groups, span // 2, 2, LANES)).reshape(groups * span, LANES)
     best = pl.pallas_call(
         score,
         out_shape=jax.ShapeDtypeStruct((groups, LANES), jnp.float32),
@@ -169,7 +173,7 @@
         compiler_params=params,
         name="score_rows",
     )(got)
-    back = lax.all_to_all(best, "grp", split_axis=0, concat_axis=0, tiled=True)
+    back = exchange(best)
     out = pl.pallas_call(
         pick,
         out_shape=jax.ShapeDtypeStruct((1, rows), jnp.float32),

time: 87.8 us -> 79.9 us (0.910)
  blocking collectives: 84.2 us -> 76.4 us
    all_to_all x2, blocking collectives: 84.2 us -> 76.4 us  [exchange(): lax.all_to_all(pieces, 'grp', split_axis=0, concat_axis=0, axis_index_gro...]
where the time goes in v4:
time: 79.9 us; the launch traced here: 79.7 us
  blocking collectives  76.4 us (96%)
  Pallas kernels  3.36 us (4%)
    all_to_all x2, blocking collectives, exchange(): lax.all_to_all(pieces, 'grp', split_axis=0, concat_axis=0, axis_index_gro...  76.4 us
    pallas_call x1, Pallas kernels, local(): pl.pallas_call(pack, in_specs=[pl.BlockSpec(memory_space=pltpu.HBM)] * 3,...  1.73 us

profile of v4, /device:TPU:6, one launch (start us, length us, event | category | flops | bytes accessed | tf_op | source)
XLA Modules:
  0.0 79.7 jit_solution(12697040662282968719)
XLA Ops:
  0.0 1.7 %pack_rows.1 = (bf16[3200,128]{1,0:T(8,128)(2,1)S(1)}, s32[1,256]{1,0:T(1,128)S(1)}) custom-call(bf16[256,768]{1,0:T(8,128)(2,1)} %refs_0_.1, s32[1,256]{1,0:T(1,128)} %bitcast.13, s32[1,256]{1,0:T(1,128)} %bitcast.14), custom_call_target="tpu_custom_call" | custom-call | tf_op jit(solution)/shard_map/pack_rows/pallas_call | solution.py:151
  1.7 57.2 %all_to_all.16 = bf16[64,25,2,128]{3,2,1,0:T(2,128)(2,1)S(1)} all-to-all(bf16[64,25,2,128]{3,2,1,0:T(2,128)(2,1)S(1)} %bitcast.10), channel_id=1, replica_groups={{38,39,40,41,42,43,44,45,46,47,48,49,50,51,52,53,54,55,56,57,58,59,60,6..., dimensions={0} | all-to-all | bytes 1638400 | tf_op jit(solution)/shard_map/all_to_all | solution.py:147
  59.0 0.9 %score_rows.1 = f32[64,128]{1,0:T(8,128)S(1)} custom-call(bf16[3200,128]{1,0:T(8,128)(2,1)S(1)} %bitcast.9), custom_call_target="tpu_custom_call" | custom-call | tf_op jit(solution)/shard_map/score_rows/pallas_call | solution.py:169
  59.9 19.1 %all_to_all.17 = f32[64,1,128]{2,1,0:T(1,128)S(1)} all-to-all(f32[64,1,128]{2,1,0:T(1,128)S(1)} %bitcast.12), channel_id=1, replica_groups={{38,39,40,41,42,43,44,45,46,47,48,49,50,51,52,53,54,55,56,57,58,59,60,6..., dimensions={0} | all-to-all | bytes 65536 | tf_op jit(solution)/shard_map/all_to_all | solution.py:147
  79.0 0.7 pick_rows.1

commit v5 on v4

--- a/solution.py
+++ b/solution.py
@@ -49,13 +49,16 @@
     copies[0].wait()
     slot_row = slots_of(cluster_ref[...], clusters, slot_cap)
     slot_ref[...] = slot_row
-    place = one_hot_bf16(lax.broadcasted_iota(jnp.int32, (groups * slots, rows), 0) == slot_row)
+    owner_row = slot_row // slots
+    inner_row = slot_row - owner_row * slots
+    place = one_hot_bf16(
+        lax.broadcasted_iota(jnp.int32, (slots * groups, rows), 0) == inner_row * groups + owner_row
+    )
     copies[1].wait()
     rank_row = rank_ref[...]
     high = rank_row // DIGIT
-    owner_row = slot_row // slots
     owned = lax.broadcasted_iota(jnp.int32, (groups, rows), 0) == owner_row
-    lane = one_hot_bf16(lax.broadcasted_iota(jnp.int32, (LANES, rows), 0) == slot_row - owner_row * slots)
+    lane = one_hot_bf16(lax.broadcasted_iota(jnp.int32, (LANES, rows), 0) == inner_row)
     for line, digit in enumerate((high + 1, rank_row - high * DIGIT)):
         digits = jnp.where(owned, digit, 0).astype(jnp.float32).astype(jnp.bfloat16)
         lines_ref[pl.ds(span - 2 + line, groups, stride=span), :] = lax.dot_general(
@@ -65,10 +68,10 @@
     floats = rows_ref[...].astype(jnp.float32)
     unit = (floats * lax.rsqrt(jnp.sum(floats * floats, axis=1, keepdims=True) + 1e-06)).astype(jnp.bfloat16)
     placed = jnp.dot(place, unit, preferred_element_type=jnp.float32)
-    for group in range(groups):
+    for slot in range(slots):
         for block in range(features // LANES):
-            lines_ref[group * span + block * slots : group * span + (block + 1) * slots, :] = placed[
-                group * slots : (group + 1) * slots, block * LANES : (block + 1) * LANES
+            lines_ref[pl.ds(block * slots + slot, groups, stride=span), :] = placed[
+                slot * groups : (slot + 1) * groups, block * LANES : (block + 1) * LANES
             ]
     send_ref[...] = lines_ref[...].astype(jnp.bfloat16)
 
@@ -78,38 +81,38 @@
     count = groups * slots
     span = lines_of(slots, features)
     lines_ref[...] = got_ref[...].astype(jnp.float32)
-    unit = jnp.concatenate(
-        [
-            jnp.concatenate(
-                [
-                    lines_ref[group * span + block * slots : group * span + (block + 1) * slots, :]
-                    for group in range(groups)
-                ],
-                axis=0,
-            ).astype(jnp.bfloat16)
-            for block in range(features // LANES)
-        ],
-        axis=1,
-    )
-    high = lines_ref[pl.ds(span - 2, groups, stride=span), :]
+    high = lines_ref[pl.ds(span - 2, groups, stride=span), :] * DIGIT
     low = lines_ref[pl.ds(span - 1, groups, stride=span), :]
-    spread = lax.broadcasted_iota(jnp.int32, (count, LANES), 1) == lax.broadcasted_iota(jnp.int32, (count, LANES), 0) % slots
-    rank = (high * DIGIT + low).reshape(groups, 1, LANES)
-    rank = jnp.broadcast_to(rank, (groups, slots, LANES)).reshape(count, LANES)
-    rank_col = jnp.sum(jnp.where(spread, rank, 0.0), axis=1, keepdims=True)
-    lane = lax.broadcasted_iota(jnp.int32, (LANES, count), 0) == lax.broadcasted_iota(jnp.int32, (LANES, count), 1) % slots
-    spread_row = jnp.dot(
-        high.astype(jnp.bfloat16), one_hot_bf16(lane) * DIGIT, preferred_element_type=jnp.float32
-    ) + jnp.dot(low.astype(jnp.bfloat16), one_hot_bf16(lane), preferred_element_type=jnp.float32)
-    mine = lax.broadcasted_iota(jnp.int32, (groups, count), 0) == lax.broadcasted_iota(jnp.int32, (groups, count), 1) // slots
-    rank_row = jnp.sum(jnp.where(mine, spread_row, 0.0), axis=0, keepdims=True)
-    products = lax.dot_general(unit, unit, (((1,), (1,)), ((), ())), preferred_element_type=jnp.float32)
-    cluster_row = lax.broadcasted_iota(jnp.int32, (1, count), 1) % slots // slot_cap
-    cluster_col = lax.broadcasted_iota(jnp.int32, (count, 1), 0) % slots // slot_cap
-    rank_row = jnp.where(rank_row < DIGIT, jnp.float32(1e9), rank_row)
-    allowed = (rank_row < rank_col) & (cluster_row == cluster_col)
-    best = jnp.max(jnp.where(allowed, products, jnp.float32(-1.0)), axis=1, keepdims=True)
-    best_ref[...] = jnp.sum(jnp.where(spread, best, 0.0).reshape(groups, slots, LANES), axis=1)
+    lane = lax.broadcasted_iota(jnp.int32, (groups, LANES), 1)
+    ones = jnp.ones((LANES, LANES), jnp.bfloat16)
+    dims = (((1,), (1,)), ((), ()))
+    best_lines = jnp.zeros((groups, LANES), jnp.float32)
+    for cluster in range(CLUS_DEV):
+        own_slots = range(cluster * slot_cap, (cluster + 1) * slot_cap)
+        unit = jnp.concatenate(
+            [
+                jnp.concatenate(
+                    [lines_ref[pl.ds(block * slots + slot, groups, stride=span), :] for slot in own_slots], axis=0
+                ).astype(jnp.bfloat16)
+                for block in range(features // LANES)
+            ],
+            axis=1,
+        )
+        products = lax.dot_general(unit, unit, dims, preferred_element_type=jnp.float32)
+        rank_col = jnp.zeros((slot_cap * groups, LANES), jnp.float32)
+        rank_row = jnp.zeros((LANES, slot_cap * groups), jnp.float32)
+        for digit in (high, low):
+            own = jnp.concatenate([jnp.where(lane == slot, digit, 0.0) for slot in own_slots], axis=0)
+            own = own.astype(jnp.bfloat16)
+            rank_col += lax.dot_general(own, ones, dims, preferred_element_type=jnp.float32)
+            rank_row += lax.dot_general(ones, own, dims, preferred_element_type=jnp.float32)
+        rank_row = rank_row[0:1, :]
+        rank_row = jnp.where(rank_row < DIGIT, jnp.float32(1e9), rank_row)
+        allowed = rank_row < rank_col[:, 0:1]
+        best = jnp.max(jnp.where(allowed, products, jnp.float32(-1.0)), axis=1, keepdims=True)
+        for place, slot in enumerate(own_slots):
+            best_lines = jnp.where(lane == slot, best[place * groups : (place + 1) * groups, :], best_lines)
+    best_ref[...] = best_lines
 
 
 def pick_kernel(slots, back_ref, slot_ref, out_ref):

time: 79.9 us -> 79.7 us (level)
  no operation moved by 1% of the time
where the time goes in v5:
time: 79.7 us; the launch traced here: 79.5 us
  blocking collectives  76.4 us (96%)
  Pallas kernels  3.1 us (4%)
    all_to_all x2, blocking collectives, exchange(): lax.all_to_all(pieces, 'grp', split_axis=0, concat_axis=0, axis_index_gro...  76.4 us
    pallas_call x1, Pallas kernels, local(): pl.pallas_call(pack, in_specs=[pl.BlockSpec(memory_space=pltpu.HBM)] * 3,...  1.7 us

profile of v5, /device:TPU:6, one launch (start us, length us, event | category | flops | bytes accessed | tf_op | source)
XLA Modules:
  0.0 79.5 jit_solution(5280986503493347892)
XLA Ops:
  0.0 1.7 %pack_rows.1 = (bf16[3200,128]{1,0:T(8,128)(2,1)S(1)}, s32[1,256]{1,0:T(1,128)S(1)}) custom-call(bf16[256,768]{1,0:T(8,128)(2,1)} %refs_0_.1, s32[1,256]{1,0:T(1,128)} %bitcast.13, s32[1,256]{1,0:T(1,128)} %bitcast.14), custom_call_target="tpu_custom_call" | custom-call | tf_op jit(solution)/shard_map/pack_rows/pallas_call | solution.py:154
  1.7 57.2 %all_to_all.16 = bf16[64,25,2,128]{3,2,1,0:T(2,128)(2,1)S(1)} all-to-all(bf16[64,25,2,128]{3,2,1,0:T(2,128)(2,1)S(1)} %bitcast.10), channel_id=1, replica_groups={{38,39,40,41,42,43,44,45,46,47,48,49,50,51,52,53,54,55,56,57,58,59,60,6..., dimensions={0} | all-to-all | bytes 1638400 | tf_op jit(solution)/shard_map/all_to_all | solution.py:150
  59.0 0.7 score_rows.1
  59.6 19.1 %all_to_all.17 = f32[64,1,128]{2,1,0:T(1,128)S(1)} all-to-all(f32[64,1,128]{2,1,0:T(1,128)S(1)} %bitcast.12), channel_id=1, replica_groups={{38,39,40,41,42,43,44,45,46,47,48,49,50,51,52,53,54,55,56,57,58,59,60,6..., dimensions={0} | all-to-all | bytes 65536 | tf_op jit(solution)/shard_map/all_to_all | solution.py:150
  78.8 0.7 pick_rows.1

commit v6 on v5

--- a/solution.py
+++ b/solution.py
@@ -8,7 +8,17 @@
 CLUS_DEV = 2
 DIGIT = 128
 LANES = 128
-FIRST = 38
+RINGS = (16, 4)
+FIRST = (10, 2)
+
+
+def order_of_group():
+    def distance(place):
+        steps = (abs(at - first) for at, first in zip(divmod(place, RINGS[1]), FIRST))
+        return sum(min(step, ring - step) for step, ring in zip(steps, RINGS))
+
+    places = range(RINGS[0] * RINGS[1])
+    return sorted(places, key=lambda place: (distance(place) > 0, -distance(place), place))
 
 
 def lines_of(slots, features):
@@ -73,14 +83,14 @@
             lines_ref[pl.ds(block * slots + slot, groups, stride=span), :] = placed[
                 slot * groups : (slot + 1) * groups, block * LANES : (block + 1) * LANES
             ]
-    send_ref[...] = lines_ref[...].astype(jnp.bfloat16)
+    send_ref[...] = lines_ref[: groups * span, :].astype(jnp.bfloat16)
 
 
 def score_kernel(slot_cap, groups, features, got_ref, best_ref, lines_ref):
     slots = CLUS_DEV * slot_cap
     count = groups * slots
     span = lines_of(slots, features)
-    lines_ref[...] = got_ref[...].astype(jnp.float32)
+    lines_ref[: groups * span, :] = got_ref[...].astype(jnp.float32)
     high = lines_ref[pl.ds(span - 2, groups, stride=span), :] * DIGIT
     low = lines_ref[pl.ds(span - 1, groups, stride=span), :]
     lane = lax.broadcasted_iota(jnp.int32, (groups, LANES), 1)
@@ -144,13 +154,13 @@
     def pick(*refs):
         pick_kernel(slots, *refs)
 
-    order = [[(FIRST + place) % groups for place in range(groups)]]
+    order = [order_of_group()]
 
     def exchange(pieces):
         return lax.all_to_all(pieces, "grp", split_axis=0, concat_axis=0, axis_index_groups=order, tiled=True)
 
     span = lines_of(slots, features)
-    lines = pltpu.VMEM((groups * span, LANES), jnp.float32)
+    lines = pltpu.VMEM((groups * span + 64, LANES), jnp.float32)
     send, slot_row = pl.pallas_call(
         pack,
         in_specs=[pl.BlockSpec(memory_space=pltpu.HBM)] * 3,

time: 79.7 us -> 79.1 us (level)
  no operation moved by 1% of the time
where the time goes in v6:
time: 79.1 us; the launch traced here: 78.9 us
  blocking collectives  75.8 us (96%)
  Pallas kernels  3.1 us (4%)
    all_to_all x2, blocking collectives, exchange(): lax.all_to_all(pieces, 'grp', split_axis=0, concat_axis=0, axis_index_gro...  75.8 us
    pallas_call x1, Pallas kernels, local(): pl.pallas_call(pack, in_specs=[pl.BlockSpec(memory_space=pltpu.HBM)] * 3,...  1.7 us

profile of v6, /device:TPU:6, one launch (start us, length us, event | category | flops | bytes accessed | tf_op | source)
XLA Modules:
  0.0 78.9 jit_solution(11776776064377825200)
XLA Ops:
  0.0 1.7 %pack_rows.1 = (bf16[3200,128]{1,0:T(8,128)(2,1)S(1)}, s32[1,256]{1,0:T(1,128)S(1)}) custom-call(bf16[256,768]{1,0:T(8,128)(2,1)} %refs_0_.1, s32[1,256]{1,0:T(1,128)} %bitcast.13, s32[1,256]{1,0:T(1,128)} %bitcast.14), custom_call_target="tpu_custom_call" | custom-call | tf_op jit(solution)/shard_map/pack_rows/pallas_call | solution.py:164
  1.7 57.6 %all_to_all.16 = bf16[64,25,2,128]{3,2,1,0:T(2,128)(2,1)S(1)} all-to-all(bf16[64,25,2,128]{3,2,1,0:T(2,128)(2,1)S(1)} %bitcast.10), channel_id=1, replica_groups={{42,8,4,9,11,12,0,5,7,10,13,15,16,1,3,6,14,17,19,20,60,2,18,21,23,24,56..., dimensions={0} | all-to-all | bytes 1638400 | tf_op jit(solution)/shard_map/all_to_all | solution.py:160
  59.3 0.7 score_rows.1
  60.0 18.2 %all_to_all.17 = f32[64,1,128]{2,1,0:T(1,128)S(1)} all-to-all(f32[64,1,128]{2,1,0:T(1,128)S(1)} %bitcast.12), channel_id=1, replica_groups={{42,8,4,9,11,12,0,5,7,10,13,15,16,1,3,6,14,17,19,20,60,2,18,21,23,24,56..., dimensions={0} | all-to-all | bytes 65536 | tf_op jit(solution)/shard_map/all_to_all | solution.py:160
  78.2 0.7 pick_rows.1

commit v7 on v6

--- a/solution.py
+++ b/solution.py
@@ -94,7 +94,7 @@
     high = lines_ref[pl.ds(span - 2, groups, stride=span), :] * DIGIT
     low = lines_ref[pl.ds(span - 1, groups, stride=span), :]
     lane = lax.broadcasted_iota(jnp.int32, (groups, LANES), 1)
-    ones = jnp.ones((LANES, LANES), jnp.bfloat16)
+    ones = jnp.ones((8, LANES), jnp.bfloat16)
     dims = (((1,), (1,)), ((), ()))
     best_lines = jnp.zeros((groups, LANES), jnp.float32)
     for cluster in range(CLUS_DEV):
@@ -109,16 +109,16 @@
             axis=1,
         )
         products = lax.dot_general(unit, unit, dims, preferred_element_type=jnp.float32)
-        rank_col = jnp.zeros((slot_cap * groups, LANES), jnp.float32)
-        rank_row = jnp.zeros((LANES, slot_cap * groups), jnp.float32)
+        rank_col = jnp.zeros((slot_cap * groups, 1), jnp.float32)
+        rank_row = jnp.zeros((8, slot_cap * groups), jnp.float32)
         for digit in (high, low):
             own = jnp.concatenate([jnp.where(lane == slot, digit, 0.0) for slot in own_slots], axis=0)
             own = own.astype(jnp.bfloat16)
-            rank_col += lax.dot_general(own, ones, dims, preferred_element_type=jnp.float32)
+            rank_col += jnp.sum(own.astype(jnp.float32), axis=1, keepdims=True)
             rank_row += lax.dot_general(ones, own, dims, preferred_element_type=jnp.float32)
         rank_row = rank_row[0:1, :]
         rank_row = jnp.where(rank_row < DIGIT, jnp.float32(1e9), rank_row)
-        allowed = rank_row < rank_col[:, 0:1]
+        allowed = rank_row < rank_col
         best = jnp.max(jnp.where(allowed, products, jnp.float32(-1.0)), axis=1, keepdims=True)
         for place, slot in enumerate(own_slots):
             best_lines = jnp.where(lane == slot, best[place * groups : (place + 1) * groups, :], best_lines)

time: 79.1 us -> 79 us (level)
  no operation moved by 1% of the time
where the time goes in v7:
time: 79 us; the launch traced here: 78.8 us
  blocking collectives  75.8 us (96%)
  Pallas kernels  3.03 us (4%)
    all_to_all x2, blocking collectives, exchange(): lax.all_to_all(pieces, 'grp', split_axis=0, concat_axis=0, axis_index_gro...  75.8 us
    pallas_call x1, Pallas kernels, local(): pl.pallas_call(pack, in_specs=[pl.BlockSpec(memory_space=pltpu.HBM)] * 3,...  1.7 us

profile of v7, /device:TPU:6, one launch (start us, length us, event | category | flops | bytes accessed | tf_op | source)
XLA Modules:
  0.0 78.8 jit_solution(102100589872161621)
XLA Ops:
  0.0 1.7 %pack_rows.1 = (bf16[3200,128]{1,0:T(8,128)(2,1)S(1)}, s32[1,256]{1,0:T(1,128)S(1)}) custom-call(bf16[256,768]{1,0:T(8,128)(2,1)} %refs_0_.1, s32[1,256]{1,0:T(1,128)} %bitcast.13, s32[1,256]{1,0:T(1,128)} %bitcast.14), custom_call_target="tpu_custom_call" | custom-call | tf_op jit(solution)/shard_map/pack_rows/pallas_call | solution.py:164
  1.7 57.6 %all_to_all.16 = bf16[64,25,2,128]{3,2,1,0:T(2,128)(2,1)S(1)} all-to-all(bf16[64,25,2,128]{3,2,1,0:T(2,128)(2,1)S(1)} %bitcast.10), channel_id=1, replica_groups={{42,8,4,9,11,12,0,5,7,10,13,15,16,1,3,6,14,17,19,20,60,2,18,21,23,24,56..., dimensions={0} | all-to-all | bytes 1638400 | tf_op jit(solution)/shard_map/all_to_all | solution.py:160
  59.3 0.6 score_rows.1
  59.9 18.2 %all_to_all.17 = f32[64,1,128]{2,1,0:T(1,128)S(1)} all-to-all(f32[64,1,128]{2,1,0:T(1,128)S(1)} %bitcast.12), channel_id=1, replica_groups={{42,8,4,9,11,12,0,5,7,10,13,15,16,1,3,6,14,17,19,20,60,2,18,21,23,24,56..., dimensions={0} | all-to-all | bytes 65536 | tf_op jit(solution)/shard_map/all_to_all | solution.py:160
  78.1 0.7 pick_rows.1

commit v8 on v7

--- a/solution.py
+++ b/solution.py
@@ -154,10 +154,18 @@
     def pick(*refs):
         pick_kernel(slots, *refs)
 
-    order = [order_of_group()]
+    first, *others = order_of_group()
+    half = len(others) // 2
+    turned = [first] + others[half:] + others[:half]
+    order = [
+        [shard * groups + place for place in (turned if shard % 2 else [first] + others)]
+        for shard in range(lax.axis_size("shard"))
+    ]
 
     def exchange(pieces):
-        return lax.all_to_all(pieces, "grp", split_axis=0, concat_axis=0, axis_index_groups=order, tiled=True)
+        return lax.all_to_all(
+            pieces, ("shard", "grp"), split_axis=0, concat_axis=0, axis_index_groups=order, tiled=True
+        )
 
     span = lines_of(slots, features)
     lines = pltpu.VMEM((groups * span + 64, LANES), jnp.float32)

time: 79 us -> 79 us (level)
  no operation moved by 1% of the time
where the time goes in v8:
time: 79 us; the launch traced here: 78.8 us
  blocking collectives  75.8 us (96%)
  Pallas kernels  3.03 us (4%)
    all_to_all x2, blocking collectives, exchange(): lax.all_to_all(pieces, ('shard', 'grp'), split_axis=0, concat_axis=0, axi...  75.8 us
    pallas_call x1, Pallas kernels, local(): pl.pallas_call(pack, in_specs=[pl.BlockSpec(memory_space=pltpu.HBM)] * 3,...  1.7 us

profile of v8, /device:TPU:6, one launch (start us, length us, event | category | flops | bytes accessed | tf_op | source)
XLA Modules:
  0.0 78.8 jit_solution(5204269419709268874)
XLA Ops:
  0.0 1.7 %pack_rows.1 = (bf16[3200,128]{1,0:T(8,128)(2,1)S(1)}, s32[1,256]{1,0:T(1,128)S(1)}) custom-call(bf16[256,768]{1,0:T(8,128)(2,1)} %refs_0_.1, s32[1,256]{1,0:T(1,128)} %bitcast.13, s32[1,256]{1,0:T(1,128)} %bitcast.14), custom_call_target="tpu_custom_call" | custom-call | tf_op jit(solution)/shard_map/pack_rows/pallas_call | solution.py:172
  1.7 57.5 %all_to_all.16 = bf16[64,25,2,128]{3,2,1,0:T(2,128)(2,1)S(1)} all-to-all(bf16[64,25,2,128]{3,2,1,0:T(2,128)(2,1)S(1)} %bitcast.10), channel_id=1, replica_groups={{42,8,4,9,11,12,0,5,7,10,13,15,16,1,3,6,14,17,19,20,60,2,18,21,23,24,56..., dimensions={0} | all-to-all | bytes 1638400 | tf_op jit(solution)/shard_map/all_to_all | solution.py:166
  59.2 0.6 score_rows.1
  59.8 18.3 %all_to_all.17 = f32[64,1,128]{2,1,0:T(1,128)S(1)} all-to-all(f32[64,1,128]{2,1,0:T(1,128)S(1)} %bitcast.12), channel_id=1, replica_groups={{42,8,4,9,11,12,0,5,7,10,13,15,16,1,3,6,14,17,19,20,60,2,18,21,23,24,56..., dimensions={0} | all-to-all | bytes 65536 | tf_op jit(solution)/shard_map/all_to_all | solution.py:166
  78.1 0.7 pick_rows.1

commit v9 on v7

--- a/solution.py
+++ b/solution.py
@@ -56,6 +56,7 @@
     ]
     for copy in copies:
         copy.start()
+    copies[1].wait()
     copies[0].wait()
     slot_row = slots_of(cluster_ref[...], clusters, slot_cap)
     slot_ref[...] = slot_row
@@ -64,7 +65,6 @@
     place = one_hot_bf16(
         lax.broadcasted_iota(jnp.int32, (slots * groups, rows), 0) == inner_row * groups + owner_row
     )
-    copies[1].wait()
     rank_row = rank_ref[...]
     high = rank_row // DIGIT
     owned = lax.broadcasted_iota(jnp.int32, (groups, rows), 0) == owner_row

time: 79 us -> 79 us (level)
  no operation moved by 1% of the time
where the time goes in v9:
time: 79 us; the launch traced here: 78.8 us
  blocking collectives  75.8 us (96%)
  Pallas kernels  3.03 us (4%)
    all_to_all x2, blocking collectives, exchange(): lax.all_to_all(pieces, 'grp', split_axis=0, concat_axis=0, axis_index_gro...  75.8 us
    pallas_call x1, Pallas kernels, local(): pl.pallas_call(pack, in_specs=[pl.BlockSpec(memory_space=pltpu.HBM)] * 3,...  1.7 us

profile of v9, /device:TPU:6, one launch (start us, length us, event | category | flops | bytes accessed | tf_op | source)
XLA Modules:
  0.0 78.8 jit_solution(11833403164929220609)
XLA Ops:
  0.0 1.7 %pack_rows.1 = (bf16[3200,128]{1,0:T(8,128)(2,1)S(1)}, s32[1,256]{1,0:T(1,128)S(1)}) custom-call(bf16[256,768]{1,0:T(8,128)(2,1)} %refs_0_.1, s32[1,256]{1,0:T(1,128)} %bitcast.13, s32[1,256]{1,0:T(1,128)} %bitcast.14), custom_call_target="tpu_custom_call" | custom-call | tf_op jit(solution)/shard_map/pack_rows/pallas_call | solution.py:164
  1.7 57.6 %all_to_all.16 = bf16[64,25,2,128]{3,2,1,0:T(2,128)(2,1)S(1)} all-to-all(bf16[64,25,2,128]{3,2,1,0:T(2,128)(2,1)S(1)} %bitcast.10), channel_id=1, replica_groups={{42,8,4,9,11,12,0,5,7,10,13,15,16,1,3,6,14,17,19,20,60,2,18,21,23,24,56..., dimensions={0} | all-to-all | bytes 1638400 | tf_op jit(solution)/shard_map/all_to_all | solution.py:160
  59.3 0.6 score_rows.1
  59.9 18.2 %all_to_all.17 = f32[64,1,128]{2,1,0:T(1,128)S(1)} all-to-all(f32[64,1,128]{2,1,0:T(1,128)S(1)} %bitcast.12), channel_id=1, replica_groups={{42,8,4,9,11,12,0,5,7,10,13,15,16,1,3,6,14,17,19,20,60,2,18,21,23,24,56..., dimensions={0} | all-to-all | bytes 65536 | tf_op jit(solution)/shard_map/all_to_all | solution.py:160
  78.1 0.7 pick_rows.1

commit v10 on v8

--- a/solution.py
+++ b/solution.py
@@ -12,13 +12,13 @@
 FIRST = (10, 2)
 
 
-def order_of_group():
+def order_of_group(turn):
     def distance(place):
         steps = (abs(at - first) for at, first in zip(divmod(place, RINGS[1]), FIRST))
         return sum(min(step, ring - step) for step, ring in zip(steps, RINGS))
 
     places = range(RINGS[0] * RINGS[1])
-    return sorted(places, key=lambda place: (distance(place) > 0, -distance(place), place))
+    return sorted(places, key=lambda place: (distance(place) > 0, -distance(place), turn * place))
 
 
 def lines_of(slots, features):
@@ -154,11 +154,8 @@
     def pick(*refs):
         pick_kernel(slots, *refs)
 
-    first, *others = order_of_group()
-    half = len(others) // 2
-    turned = [first] + others[half:] + others[:half]
     order = [
-        [shard * groups + place for place in (turned if shard % 2 else [first] + others)]
+        [shard * groups + place for place in order_of_group(-1 if shard % 2 else 1)]
         for shard in range(lax.axis_size("shard"))
     ]
 

time: 79 us -> 79 us (level)
  no operation moved by 1% of the time
where the time goes in v10:
time: 79 us; the launch traced here: 78.8 us
  blocking collectives  75.8 us (96%)
  Pallas kernels  3.03 us (4%)
    all_to_all x2, blocking collectives, exchange(): lax.all_to_all(pieces, ('shard', 'grp'), split_axis=0, concat_axis=0, axi...  75.8 us
    pallas_call x1, Pallas kernels, local(): pl.pallas_call(pack, in_specs=[pl.BlockSpec(memory_space=pltpu.HBM)] * 3,...  1.7 us

profile of v10, /device:TPU:6, one launch (start us, length us, event | category | flops | bytes accessed | tf_op | source)
XLA Modules:
  0.0 78.8 jit_solution(4766630513625467184)
XLA Ops:
  0.0 1.7 %pack_rows.1 = (bf16[3200,128]{1,0:T(8,128)(2,1)S(1)}, s32[1,256]{1,0:T(1,128)S(1)}) custom-call(bf16[256,768]{1,0:T(8,128)(2,1)} %refs_0_.1, s32[1,256]{1,0:T(1,128)} %bitcast.13, s32[1,256]{1,0:T(1,128)} %bitcast.14), custom_call_target="tpu_custom_call" | custom-call | tf_op jit(solution)/shard_map/pack_rows/pallas_call | solution.py:169
  1.7 57.6 %all_to_all.16 = bf16[64,25,2,128]{3,2,1,0:T(2,128)(2,1)S(1)} all-to-all(bf16[64,25,2,128]{3,2,1,0:T(2,128)(2,1)S(1)} %bitcast.10), channel_id=1, replica_groups={{42,8,4,9,11,12,0,5,7,10,13,15,16,1,3,6,14,17,19,20,60,2,18,21,23,24,56..., dimensions={0} | all-to-all | bytes 1638400 | tf_op jit(solution)/shard_map/all_to_all | solution.py:163
  59.3 0.6 score_rows.1
  59.9 18.1 %all_to_all.17 = f32[64,1,128]{2,1,0:T(1,128)S(1)} all-to-all(f32[64,1,128]{2,1,0:T(1,128)S(1)} %bitcast.12), channel_id=1, replica_groups={{42,8,4,9,11,12,0,5,7,10,13,15,16,1,3,6,14,17,19,20,60,2,18,21,23,24,56..., dimensions={0} | all-to-all | bytes 65536 | tf_op jit(solution)/shard_map/all_to_all | solution.py:163
  78.1 0.7 pick_rows.1
